TPU v7x, 128 devices: a whole 4x4x4 slice. The times are simulated.
128 devices in a mesh: samp: 16 (over x_hi, z, core), par: 8 (over x_lo, y).
Axes of the slice: x: 4 (x_hi: 2, x_lo: 2; x = x_hi * 2 + x_lo), y: 4, z: 4, core: 2. Of those that a mesh axis runs over, the one named last changes fastest.
Arguments:
- jacobian: bfloat16 [65536, 16384], P(('samp', 'par')), may hold values from -6 to 6
- energy: float32 [65536], P('samp'), may hold values from -6 to 6
Outputs:
- update: float32 [16384], P('par')
- residual: float32 [16384], P('par')
All inputs are finite; a program needn't handle non-finite values.
Results may differ from a plain program's by a relative error of at most 0.033.
Values may be sent and summed in bfloat16 or wider, within the bound.
A program may use at most 128 MiB of HBM per device.

v0:
```python
import jax
import jax.numpy as jnp
from jax import lax
from jax.sharding import PartitionSpec as P

ITERS = 3


damping = 0.05


def body(jacobian, energy):
    count = jacobian.shape[0]
    total = count * lax.axis_size("samp") * lax.axis_size("par")
    start = lax.axis_index("par") * count
    mine = lax.dynamic_slice_in_dim(energy, start, count, 0)
    deviation = mine.astype(jnp.bfloat16)
    force = (
        lax.psum(jnp.dot(deviation, jacobian, preferred_element_type=jnp.float32), ("samp", "par"))
        / total
    )
    update = jnp.zeros_like(force)
    residual = force
    direction = force
    norm_now = jnp.sum(residual * residual)
    for step in range(ITERS):
        narrow = direction.astype(jnp.bfloat16)
        inner = jnp.dot(jacobian, narrow, preferred_element_type=jnp.float32).astype(jnp.bfloat16)
        back = lax.psum(
            jnp.dot(inner, jacobian, preferred_element_type=jnp.float32), ("samp", "par")
        )
        image = back / total + damping * direction
        alpha = norm_now / jnp.sum(direction * image)
        update = update + alpha * direction
        residual = residual - alpha * image
        norm_next = jnp.sum(residual * residual)
        direction = residual + norm_next / norm_now * direction
        norm_now = norm_next
    width = force.shape[0] // lax.axis_size("par")
    offset = lax.axis_index("par") * width
    return (
        lax.dynamic_slice_in_dim(update, offset, width, 0),
        lax.dynamic_slice_in_dim(residual, offset, width, 0),
    )


def solution(mesh):
    return jax.shard_map(
        body,
        mesh=mesh,
        in_specs=(P(("samp", "par"), None), P("samp")),
        out_specs=(P("par"), P("par")),
        check_vma=False,
    )
```

profile of v0, /device:TPU:1, one launch (start us, length us, event | category | flops | bytes accessed | tf_op | source)
XLA Modules:
  0.0 642.0 jit_solution(12160243628257740363)
XLA Ops:
  7.2 0.0 all-reduce.5.cloned.1.call-start
  7.2 0.8 dynamic_slice.33
  8.0 8.7 %fusion.4 = f32[1,16384]{1,0:T(1,128)} fusion(bf16[512,1]{0,1:T(2,128)(2,1)S(1)} %reshape.4, bf16[512,16384]{1,0:T(8,128)(2,1)} %param.2), kind=kOutput, calls=%fused_computation.24 | convolution fusion | flops 16777216 | bytes 16843776 | tf_op jit(solution)/shard_map/dot_general | solution.py:19
  16.7 0.0 all-reduce.5.cloned.1.call-update
  16.7 0.0 all-reduce.7.cloned.1.call-start
  16.7 141.1 %all-reduce.5.cloned.1.call-done = f32[16384]{0:T(1024)} async-done(((f32[16384]{0:T(1024)}), f32[16384]{0:T(1024)}) %all-reduce.5.cloned.1.call-update) | async-done | bytes 65552 | tf_op jit(solution)/shard_map/psum | solution.py:19
  157.8 0.8 multiply_convert_fusion
  158.7 0.0 copy-start
  158.7 10.2 %fusion.5 = f32[1,512]{1,0:T(1,128)S(1)} fusion(bf16[16384,1]{0,1:T(2,128)(2,1)S(1)} %reshape.6, bf16[512,16384]{1,0:T(8,128)(2,1)} %param.2), kind=kOutput, calls=%fused_computation.25 | convolution fusion | flops 16777216 | bytes 16812032 | tf_op jit(solution)/shard_map/dot_general | solution.py:28
  169.0 8.7 %fusion.6 = f32[1,16384]{1,0:T(1,128)} fusion(bf16[512,1]{0,1:T(2,128)(2,1)S(1)} %reshape.8, bf16[512,16384]{1,0:T(8,128)(2,1)} %param.2), kind=kOutput, calls=%fused_computation.26 | convolution fusion | flops 16777216 | bytes 16843776 | tf_op jit(solution)/shard_map/dot_general | solution.py:30
  177.6 0.0 all-reduce.7.cloned.1.call-update
  177.7 0.2 all-reduce.9.cloned.1.call-start
  177.9 134.5 %all-reduce.7.cloned.1.call-done = f32[16384]{0:T(1024)} async-done(((f32[16384]{0:T(1024)}), f32[16384]{0:T(1024)}) %all-reduce.7.cloned.1.call-update) | async-done | bytes 65552 | tf_op jit(solution)/shard_map/psum | solution.py:29
  312.4 0.0 copy-done
  312.4 1.5 multiply_reduce_fusion.4
  315.2 1.5 multiply_reduce_fusion.3
  318.0 0.9 fusion.3
  318.9 0.0 copy-start.1
  318.9 10.2 %fusion.7 = f32[1,512]{1,0:T(1,128)S(1)} fusion(bf16[16384,1]{0,1:T(2,128)(2,1)S(1)} %reshape.10, bf16[512,16384]{1,0:T(8,128)(2,1)} %param.2), kind=kOutput, calls=%fused_computation.27 | convolution fusion | flops 16777216 | bytes 16812032 | tf_op jit(solution)/shard_map/dot_general | solution.py:28
  329.2 8.7 %fusion.8 = f32[1,16384]{1,0:T(1,128)} fusion(bf16[512,1]{0,1:T(2,128)(2,1)S(1)} %reshape.12, bf16[512,16384]{1,0:T(8,128)(2,1)} %param.2), kind=kOutput, calls=%fused_computation.28 | convolution fusion | flops 16777216 | bytes 16843776 | tf_op jit(solution)/shard_map/dot_general | solution.py:30
  337.9 0.0 all-reduce.9.cloned.1.call-update
  337.9 0.3 all-reduce.11.cloned.1.call-start
  338.2 134.5 %all-reduce.9.cloned.1.call-done = f32[16384]{0:T(1024)} async-done(((f32[16384]{0:T(1024)}), f32[16384]{0:T(1024)}) %all-reduce.9.cloned.1.call-update) | async-done | bytes 65552 | tf_op jit(solution)/shard_map/psum | solution.py:29
  472.7 1.5 multiply_reduce_fusion.2
  475.5 0.0 copy-done.1
  475.5 1.5 multiply_reduce_fusion.1
  478.3 10.2 %fusion.9 = f32[1,512]{1,0:T(1,128)S(1)} fusion(bf16[16384,1]{0,1:T(2,128)(2,1)S(1)} %reshape.14, bf16[512,16384]{1,0:T(8,128)(2,1)} %param.2), kind=kOutput, calls=%fused_computation.29 | convolution fusion | flops 16777216 | bytes 16812032 | tf_op jit(solution)/shard_map/dot_general | solution.py:28
  488.6 8.7 %fusion.10 = f32[1,16384]{1,0:T(1,128)} fusion(bf16[512,1]{0,1:T(2,128)(2,1)S(1)} %reshape.16, bf16[512,16384]{1,0:T(8,128)(2,1)} %param.2), kind=kOutput, calls=%fused_computation.30 | convolution fusion | flops 16777216 | bytes 16843776 | tf_op jit(solution)/shard_map/dot_general | solution.py:30
  497.2 0.0 all-reduce.11.cloned.1.call-update
  497.3 134.8 %all-reduce.11.cloned.1.call-done = f32[16384]{0:T(1024)} async-done(((f32[16384]{0:T(1024)}), f32[16384]{0:T(1024)}) %all-reduce.11.cloned.1.call-update) | async-done | bytes 65552 | tf_op jit(solution)/shard_map/psum | solution.py:29
  632.0 1.5 multiply_add_fusion
  634.8 0.6 dynamic-slice_subtract_fusion
  (11 shorter events, 0.2 us)
Async XLA Ops:
  7.2 150.7 %all-reduce.5.cloned.1.call-start = ((), (), s32[]{:S(2)}) async-start(), calls=%async_computation | async-start | bytes 131072 | tf_op jit(solution)/shard_map/psum | solution.py:19
  16.7 295.7 %all-reduce.7.cloned.1.call-start = ((), (), s32[]{:S(2)}) async-start(), calls=%async_computation.1 | async-start | bytes 131072 | tf_op jit(solution)/shard_map/psum | solution.py:29
  158.7 153.7 %copy-start = (f32[16384]{0:T(1024)S(1)}, f32[16384]{0:T(1024)}, u32[]{:S(2)}) copy-start(f32[16384]{0:T(1024)} %all-reduce.5.cloned.1.call-done) | copy-start | bytes 196612
  177.7 295.0 %all-reduce.9.cloned.1.call-start = ((), (), s32[]{:S(2)}) async-start(), calls=%async_computation.2 | async-start | bytes 131072 | tf_op jit(solution)/shard_map/psum | solution.py:29
  318.9 156.5 %copy-start.1 = (f32[16384]{0:T(1024)S(1)}, f32[16384]{0:T(1024)}, u32[]{:S(2)}) copy-start(f32[16384]{0:T(1024)} %all-reduce.7.cloned.1.call-done) | copy-start | bytes 196612
  337.9 294.1 %all-reduce.11.cloned.1.call-start = ((), (), s32[]{:S(2)}) async-start(), calls=%async_computation.3 | async-start | bytes 131072 | tf_op jit(solution)/shard_map/psum | solution.py:29
Sparse Core Ops, SparseCore 0:
  16.8 140.9 all-reduce.4
  177.8 134.5 all-reduce.6
  338.0 134.5 all-reduce.8
  497.4 134.5 all-reduce.10
where the time goes:
time: 643 us; the launch traced here: 642 us
  waiting for transfers between devices  545 us (85%)
  matrix products  65.3 us (10%)
  between operations  20.5 us (3%)
  other arithmetic  9.69 us (2%)
    psum x3, waiting for transfers between devices, body(): lax.psum(jnp.dot(inner, jacobian, preferred_element_type=jnp.float32), ('...  404 us
    psum x1, waiting for transfers between devices, body(): lax.psum(jnp.dot(deviation, jacobian, preferred_element_type=jnp.float32)...  141 us
    dot_general x3, matrix products, body(): jnp.dot(jacobian, narrow, preferred_element_type=jnp.float32)  30.6 us
    dot_general x3, matrix products, body(): jnp.dot(inner, jacobian, preferred_element_type=jnp.float32)  26 us
  transfers between devices with their start and end apart: 4, of which 4 were waited for; matrix products, arithmetic and copies ran while one was open for 0% of the time, Pallas kernels for 0%

commit v1 on v0

v1 whole, which is shorter than its diff:
```python
import functools

import jax
import jax.numpy as jnp
from jax import lax
from jax.experimental import pallas as pl
from jax.experimental.pallas import tpu as pltpu
from jax.sharding import PartitionSpec as P

ITERS = 3
DAMPING = 0.05
LANES = 128
CHUNKS = 4
MESH = pl.DeviceIdType.MESH
f32, bf16 = jnp.float32, jnp.bfloat16


def coordinates():
    samp, par = lax.axis_index("samp"), lax.axis_index("par")
    x = (samp // 8) * 2 + par // 4
    return x, par % 4, (samp // 2) % 4, samp % 2


def device(x, y, z, c):
    return ((x // 2) * 8 + z * 2 + c, (x % 2) * 4 + y)


def kernel(
    total,
    energy, jac_hbm, update_out, residual_out,
    jac, part, core_out, core_in, plane, axis,
    update, residual, direction, image, wide, narrow,
    load_sem, core_send, core_recv, plane_send, plane_recv, axis_send, axis_recv,
):
    rows, params = jac.shape
    width = params // CHUNKS
    tall = width // LANES
    half = tall // 2
    x, y, z, c = coordinates()
    me = x * 4 + y
    own = c * 4 + z
    sibling = device(x, y, z, 1 - c)
    plane_peers = [
        device((x + a) % 4, (y + b) % 4, z, c) for a in range(4) for b in range(4) if a or b
    ]
    axis_peers = [device(x, y, (z + d) % 4, c) for d in (1, 2, 3)]
    axis_peers += [device(x, y, (z + d) % 4, 1 - c) for d in (1, 2, 3, 0)]

    def load(k):
        columns = pl.ds(k * width, width)
        return pltpu.make_async_copy(jac_hbm.at[:, columns], jac.at[:, columns], load_sem.at[k])

    for k in range(CHUNKS):
        load(k).start()

    barrier = pltpu.get_barrier_semaphore()
    for peer in plane_peers + axis_peers:
        pl.semaphore_signal(barrier, inc=1, device_id=peer, device_id_type=MESH)
    pl.semaphore_wait(barrier, len(plane_peers) + len(axis_peers))

    def core_copy(p, k):
        return pltpu.make_async_remote_copy(
            core_out.at[p, k], core_in.at[p, k], core_send.at[p, k], core_recv.at[p, k],
            device_id=sibling, device_id_type=MESH,
        )

    def slot_copy(buffer, send, recv, p, k, slot, peer):
        return pltpu.make_async_remote_copy(
            buffer.at[p, k, slot], buffer.at[p, k, slot], send.at[p, k], recv.at[p, k],
            device_id=peer, device_id_type=MESH,
        )

    plane_copy = functools.partial(slot_copy, plane, plane_send, plane_recv)
    axis_copy = functools.partial(slot_copy, axis, axis_send, axis_recv)
    plane_all, axis_all = pl.ds(0, len(plane_peers)), pl.ds(0, len(axis_peers))

    def to_plane(p, k):
        core_copy(p, k).wait_recv()
        mine = part[pl.ds(k * tall + c * half, half)] + core_in[p, k].astype(f32)
        plane[p, k, me] = mine.astype(bf16)
        for peer in plane_peers:
            plane_copy(p, k, me, peer).start()

    def to_axis(p, k):
        plane_copy(p, k, plane_all, sibling).wait_recv()
        mine = jnp.sum(plane[p, k].astype(f32), axis=0)
        axis[p, k, own] = mine.astype(bf16)
        for peer in axis_peers:
            axis_copy(p, k, own, peer).start()

    def send_out(p, vector, first):
        for k in range(CHUNKS):
            if first:
                load(k).wait()
            product = jnp.dot(vector, jac[:, k * width : (k + 1) * width], preferred_element_type=f32)
            for i in range(tall):
                part[k * tall + i : k * tall + i + 1] = product[:1, i * LANES : (i + 1) * LANES]
            core_out[p, k] = part[pl.ds(k * tall + (1 - c) * half, half)].astype(bf16)
            core_copy(p, k).start()
            if k >= 1:
                to_plane(p, k - 1)
        to_plane(p, CHUNKS - 1)
        for k in range(CHUNKS):
            to_axis(p, k)

    def arrive(p, k):
        axis_copy(p, k, axis_all, sibling).wait_recv()
        for h in range(2):
            value = jnp.sum(axis[p, k, h * 4 : h * 4 + 4].astype(f32), axis=0)
            image[k * tall + h * half : k * tall + (h + 1) * half] = value * (1.0 / total)

    def forward(k):
        value = image[k * tall : (k + 1) * tall]
        high = value.astype(bf16).astype(f32)
        wide[0] = high
        wide[1] = value - high
        for i in range(tall):
            columns = slice(i * LANES, (i + 1) * LANES)
            narrow[0:1, columns] = wide[0, i : i + 1]
            narrow[1:2, columns] = wide[1, i : i + 1]
        out = lax.dot_general(
            narrow[...].astype(bf16), jac[:, k * width : (k + 1) * width],
            (((1,), (1,)), ((), ())), preferred_element_type=f32,
        )
        return out[0:1] + out[1:2]

    def drain(p):
        for k in range(CHUNKS):
            core_copy(p, k).wait_send()
            plane_copy(p, k, plane_all, sibling).wait_send()
            axis_copy(p, k, axis_all, sibling).wait_send()

    def row8(row):
        return jnp.broadcast_to(row, (8, rows)).astype(bf16)

    def scalar(value):
        return jnp.sum(value, keepdims=True)

    narrow[...] = jnp.zeros(narrow.shape, f32)
    start = lax.axis_index("par") * (rows // LANES)
    deviation = jnp.concatenate(
        [energy[pl.ds(start + i, 1), :] for i in range(rows // LANES)], axis=1
    )
    send_out(0, row8(deviation), True)
    inner = jnp.zeros((1, rows), f32)
    for k in range(CHUNKS):
        arrive(0, k)
        inner += forward(k)
    drain(0)
    force = image[...]
    residual[...] = force
    direction[...] = force
    update[...] = jnp.zeros(force.shape, f32)
    norm = scalar(force * force)

    def advance(norm):
        image[...] = image[...] + DAMPING * direction[...]
        alpha = norm / scalar(direction[...] * image[...])
        update[...] = update[...] + alpha * direction[...]
        residual[...] = residual[...] - alpha * image[...]
        return alpha

    def step(it, carry):
        norm, left, along = carry
        p = (it + 1) % 2
        send_out(p, row8(along), False)
        inner = DAMPING * along
        for k in range(CHUNKS):
            arrive(p, k)
            inner += forward(k)
        drain(p)
        alpha = advance(norm)
        new = scalar(residual[...] * residual[...])
        beta = new / norm
        direction[...] = residual[...] + beta * direction[...]
        left = left - alpha * inner
        return new, left, left + beta * along

    norm, left, along = lax.fori_loop(0, ITERS - 1, step, (norm, inner, inner))
    p = ITERS % 2
    send_out(p, row8(along), False)
    for k in range(CHUNKS):
        arrive(p, k)
    drain(p)
    advance(norm)
    mine = pl.ds(lax.axis_index("par") * update_out.shape[0], update_out.shape[0])
    update_out[...] = update[mine]
    residual_out[...] = residual[mine]


def body(jacobian, energy):
    rows, params = jacobian.shape
    total = rows * lax.axis_size("samp") * lax.axis_size("par")
    tall = params // CHUNKS // LANES
    whole = (params // LANES, LANES)
    piece = (tall // 2, LANES)
    out = jax.ShapeDtypeStruct((params // lax.axis_size("par") // LANES, LANES), f32)
    vmem = pl.BlockSpec(memory_space=pltpu.VMEM)
    dma = pltpu.SemaphoreType.DMA
    update, residual = pl.pallas_call(
        functools.partial(kernel, total),
        out_shape=(out, out),
        in_specs=[vmem, pl.BlockSpec(memory_space=pl.ANY)],
        out_specs=(vmem, vmem),
        scratch_shapes=[
            pltpu.VMEM((rows, params), bf16),
            pltpu.VMEM(whole, f32),
            pltpu.VMEM((2, CHUNKS, *piece), bf16),
            pltpu.VMEM((2, CHUNKS, *piece), bf16),
            pltpu.VMEM((2, CHUNKS, 16, *piece), bf16),
            pltpu.VMEM((2, CHUNKS, 8, *piece), bf16),
            pltpu.VMEM(whole, f32),
            pltpu.VMEM(whole, f32),
            pltpu.VMEM(whole, f32),
            pltpu.VMEM(whole, f32),
            pltpu.VMEM((2, tall, LANES), f32),
            pltpu.VMEM((8, params // CHUNKS), f32),
            dma((CHUNKS,)),
        ]
        + [dma((2, CHUNKS))] * 6,
        compiler_params=pltpu.CompilerParams(
            collective_id=0, has_side_effects=True, vmem_limit_bytes=56 * 2**20
        ),
    )(energy.reshape(-1, LANES), jacobian)
    return update.reshape(-1), residual.reshape(-1)


def solution(mesh):
    return jax.shard_map(
        body,
        mesh=mesh,
        in_specs=(P(("samp", "par"), None), P("samp")),
        out_specs=(P("par"), P("par")),
        check_vma=False,
    )
```

time: 643 us -> 71.4 us (0.11)
  waiting for transfers between devices: 545 us -> 0 us
  Pallas kernels: 0 us -> 67.9 us
  matrix products: 65.3 us -> 0 us
  between operations: 20.5 us -> 0.64 us
  other arithmetic: 9.69 us -> 0 us
    psum x4 -> x0, waiting for transfers between devices: 545 us -> none  [the longest x3 404 us: body(): lax.psum(jnp.dot(inner, jacobian, preferred_element_type=jnp.float32), ('...]
    pallas_call x0 -> x1, Pallas kernels: none -> 67.9 us  [body(): pl.pallas_call(functools.partial(kernel, total), out_shape=(out, out), in...]
    dot_general x7 -> x0, matrix products: 65.3 us -> none  [the longest x3 30.6 us: body(): jnp.dot(jacobian, narrow, preferred_element_type=jnp.float32)]
  transfers between devices with their start and end apart: 4 -> 0, of which waited for: 4 -> 0; matrix products, arithmetic and copies ran while one was open for 0% -> 0% of each run, Pallas kernels for 0% -> 0%
where the time goes in v1:
time: 71.4 us; the launch traced here: 71.1 us
  Pallas kernels  67.9 us (95%)
  local copies, waits for them, and re-layouts  2.59 us (4%)
    pallas_call x1, Pallas kernels, body(): pl.pallas_call(functools.partial(kernel, total), out_shape=(out, out), in...  67.9 us
    unnamed x2, local copies, waits for them, and re-layouts  2.59 us

profile of v1, /device:TPU:1, one launch (start us, length us, event | category | flops | bytes accessed | tf_op | source)
XLA Modules:
  0.0 71.1 jit_solution(3941723302216726058)
XLA Ops:
  0.6 67.9 %shard_map.41 = (f32[16,128]{1,0:T(8,128)}, f32[16,128]{1,0:T(8,128)}) custom-call(f32[32,128]{1,0:T(8,128)} %bitcast.3, bf16[512,16384]{1,0:T(8,128)(2,1)} %jac_hbm.1), custom_call_target="tpu_custom_call" | custom-call | tf_op jit(solution)/shard_map/pallas_call | solution.py:200
  68.5 1.3 %copy.6 = f32[2048]{0:T(1024)} copy(f32[2048]{0:T(1024)} %bitcast.5) | data formatting | bytes 16384
  69.8 1.3 %copy.7 = f32[2048]{0:T(1024)} copy(f32[2048]{0:T(1024)} %bitcast.4) | data formatting | bytes 16384

commit v2 on v1

v2 whole, which is shorter than its diff:
```python
import functools

import jax
import jax.numpy as jnp
from jax import lax
from jax.experimental import pallas as pl
from jax.experimental.pallas import tpu as pltpu
from jax.sharding import PartitionSpec as P

ITERS = 3
DAMPING = 0.05
LANES = 128
CHUNKS = 4
VECTOR_TILES = 12
MESH = pl.DeviceIdType.MESH
f32, bf16 = jnp.float32, jnp.bfloat16


def coordinates():
    samp, par = lax.axis_index("samp"), lax.axis_index("par")
    x = (samp // 8) * 2 + par // 4
    return x, par % 4, (samp // 2) % 4, samp % 2


def device(x, y, z, c):
    return ((x // 2) * 8 + z * 2 + c, (x % 2) * 4 + y)


def hops(*steps):
    return -sum(min(s, 4 - s) for s in steps)


def kernel(
    total,
    energy, jac_hbm, outs,
    jac, jac_t, part, spread, column_out, column, plane, last_out, last, scalar_column, scalar_plane,
    update, residual, direction, image, wide, narrow,
    load_sem, column_send, column_recv, plane_send, plane_recv, core_send, core_recv,
    last_send, last_recv, scalar_send, scalar_recv,
):
    rows, params = jac.shape
    width = params // CHUNKS
    tall = width // LANES
    half = tall // 2
    x, y, z, c = coordinates()
    me = x * 4 + y
    own = c * 4 + z
    sibling = device(x, y, z, 1 - c)
    plane_peers = [
        device((x + a) % 4, (y + b) % 4, z, c)
        for a, b in sorted(((a, b) for a in range(4) for b in range(4) if a or b), key=lambda s: hops(*s))
    ]
    column_peers = [
        ((c + e) % 2, device(x, y, (z + d) % 4, (c + e) % 2))
        for d, e in sorted(((d, e) for d in range(4) for e in range(2) if d or e), key=lambda s: hops(s[0]))
    ]
    scale = 1.0 / total

    def load(k):
        columns = pl.ds(pl.multiple_of(k * width, width), width)
        return pltpu.make_async_copy(jac_hbm.at[:, columns], jac.at[:, columns], load_sem.at[k])

    for k in range(CHUNKS):
        load(k).start()

    barrier = pltpu.get_barrier_semaphore()
    others = [
        device((x + a) % 4, (y + b) % 4, z, 1 - c) for a in range(4) for b in range(4) if a or b
    ]
    greeted = plane_peers + others + [peer for _, peer in column_peers]
    for peer in greeted:
        pl.semaphore_signal(barrier, inc=1, device_id=peer, device_id_type=MESH)
    pl.semaphore_wait(barrier, len(greeted))

    def copy_to(peer, source, target, send, recv):
        return pltpu.make_async_remote_copy(
            source, target, send, recv, device_id=peer, device_id_type=MESH
        )

    def column_copy(p, k, core, peer):
        return copy_to(
            peer, column_out.at[p, k, core], column.at[p, k, own], column_send.at[p, k], column_recv.at[p, k]
        )

    def column_all(p, k):
        some = column.at[p, k, pl.ds(0, 7)]
        return copy_to(sibling, some, some, column_send.at[p, k], column_recv.at[p, k])

    def plane_copy(p, k, slot, peer):
        piece = plane.at[p, k, slot]
        return copy_to(peer, piece, piece, plane_send.at[p, k], plane_recv.at[p, k])

    def plane_all(p, k):
        return plane_copy(p, k, pl.ds(0, 15), sibling)

    def core_copy(p, k):
        piece = image.at[p, pl.ds(k * tall + c * half, half)]
        return copy_to(sibling, piece, piece, core_send.at[p, k], core_recv.at[p, k])

    def each(step):
        lax.fori_loop(0, CHUNKS, lambda k, _: (step(k), 0)[1], 0)

    def multiply(k, vector):
        base = pl.multiple_of(k * width, width)
        split = tall - VECTOR_TILES
        product = jnp.dot(vector, jac[:, pl.ds(base, split * LANES)], preferred_element_type=f32)
        for i in range(split):
            part[i : i + 1] = product[:1, i * LANES : (i + 1) * LANES]
        sums = [jnp.zeros((8, LANES), f32) for _ in range(VECTOR_TILES)]
        for r in range(0, rows, 8):
            factor = spread[r : r + 8]
            for w in range(VECTOR_TILES):
                columns = pl.ds(base + (split + w) * LANES, LANES)
                sums[w] += jac[r : r + 8, columns].astype(f32) * factor
        for w in range(VECTOR_TILES):
            part[split + w : split + w + 1] = jnp.sum(sums[w], axis=0, keepdims=True)

    def transpose(first, count):
        piece = 512

        def one(i, _):
            columns = pl.ds(pl.multiple_of(i * piece, piece), piece)
            jac_t[columns, :] = jac[:, columns].T
            return 0

        lax.fori_loop(first // piece, (first + count) // piece, one, 0)

    def send_columns(p, row, first):
        vector = jnp.broadcast_to(row, (8, rows)).astype(bf16)
        whole = vector[:1].astype(f32)
        for i in range(rows // LANES):
            tile = jnp.broadcast_to(whole[:, i * LANES : (i + 1) * LANES], (LANES, LANES))
            spread[i * LANES : (i + 1) * LANES] = tile.T

        def chunk(k):
            if first:
                load(k).wait()
            multiply(k, vector)
            column_out[p, k, 0] = part[:half].astype(bf16)
            column_out[p, k, 1] = part[half:].astype(bf16)
            column[p, k, own] = column_out[p, k, c]
            for core, peer in column_peers:
                column_copy(p, k, core, peer).start()

        each(chunk)

    def column_sum(p, k):
        column_all(p, k).wait_recv()
        return jnp.sum(column[p, k].astype(f32), axis=0).astype(bf16)

    def send_plane(p, k):
        plane[p, k, me] = column_sum(p, k)
        for peer in plane_peers:
            plane_copy(p, k, me, peer).start()

    def forward(p, k, h):
        value = image[p, pl.ds(k * tall + h * half, half)]
        high = value.astype(bf16).astype(f32)
        wide[0] = high
        wide[1] = value - high
        for i in range(half):
            columns = slice(i * LANES, (i + 1) * LANES)
            narrow[0:1, columns] = wide[0, i : i + 1]
            narrow[1:2, columns] = wide[1, i : i + 1]
        depth = width // 2
        base = pl.multiple_of(k * width + h * depth, depth)
        out = jnp.dot(narrow[...].astype(bf16), jac_t[pl.ds(base, depth), :], preferred_element_type=f32)
        return out[0:1] + out[1:2]

    def gather(p):
        def mine(k, inner):
            plane_all(p, k).wait_recv()
            value = jnp.sum(plane[p, k].astype(f32), axis=0)
            image[p, pl.ds(k * tall + c * half, half)] = value * scale
            core_copy(p, k).start()
            return inner + forward(p, k, c)

        def theirs(k, inner):
            core_copy(p, k).wait_recv()
            return inner + forward(p, k, 1 - c)

        inner = lax.fori_loop(0, CHUNKS, mine, jnp.zeros((1, rows), f32))
        return lax.fori_loop(0, CHUNKS, theirs, inner)

    def drain(p):
        def chunk(k):
            column_all(p, k).wait_send()
            plane_all(p, k).wait_send()
            core_copy(p, k).wait_send()

        each(chunk)

    def dot(a, b):
        return jnp.sum(a * b, keepdims=True)

    narrow[...] = jnp.zeros(narrow.shape, f32)
    start = lax.axis_index("par") * (rows // LANES)
    deviation = jnp.concatenate(
        [energy[pl.ds(start + i, 1), :] for i in range(rows // LANES)], axis=1
    )
    send_columns(0, deviation, True)
    transpose(0, params // 2)
    each(functools.partial(send_plane, 0))
    transpose(params // 2, params // 2)
    inner = gather(0)
    drain(0)
    force = image[0]
    residual[...] = force
    direction[...] = force
    update[...] = jnp.zeros(force.shape, f32)
    norm = dot(force, force)

    def step(it, carry):
        norm, left, along = carry
        p = (it + 1) % 2
        send_columns(p, along, False)
        each(functools.partial(send_plane, p))
        inner = gather(p) + DAMPING * along
        drain(p)
        applied = image[p] + DAMPING * direction[...]
        alpha = norm / dot(direction[...], applied)
        update[...] = update[...] + alpha * direction[...]
        residual[...] = residual[...] - alpha * applied
        new = dot(residual[...], residual[...])
        beta = new / norm
        direction[...] = residual[...] + beta * direction[...]
        left = left - alpha * inner
        return new, left, left + beta * along

    norm, left, along = lax.fori_loop(0, ITERS - 1, step, (norm, inner, inner))

    p = ITERS % 2

    def scalar_copy(buffer, slot, stage, peer):
        piece = buffer.at[slot]
        return copy_to(peer, piece, piece, scalar_send.at[stage], scalar_recv.at[stage])

    squares = dot(along.astype(bf16).astype(f32), along)
    scalar_column[own] = jnp.broadcast_to(squares, (1, LANES))
    for _, peer in column_peers:
        scalar_copy(scalar_column, own, 0, peer).start()
    send_columns(p, along, False)
    scalar_copy(scalar_column, pl.ds(0, 7), 0, sibling).wait()
    scalar_plane[me] = jnp.sum(scalar_column[...], axis=0)
    for peer in plane_peers:
        scalar_copy(scalar_plane, me, 1, peer).start()

    def last_copy(source, slot, peer):
        return copy_to(peer, source, last.at[slot], last_send, last_recv)

    for k in range(CHUNKS):
        last_out[k] = column_sum(p, k)
        to_y = 2 * (k % 2) + c
        for to_x in (k // 2, k // 2 + 2):
            last_copy(last_out.at[k], me, device(to_x, to_y, z, 1 - c)).start()
            local = jnp.logical_and(x == to_x, y == to_y)

            @pl.when(jnp.logical_not(local))
            def _():
                last_copy(last_out.at[k], me, device(to_x, to_y, z, c)).start()

            @pl.when(local)
            def _():
                last[me] = last_out[k]

    scalar_copy(scalar_plane, pl.ds(0, 15), 1, sibling).wait()
    squares = jnp.sum(scalar_plane[...], axis=0)[:, :1] * scale
    alpha = norm / (squares + DAMPING * dot(direction[...], direction[...]))

    def last_all(count):
        return last_copy(last.at[pl.ds(0, count)], pl.ds(0, count), sibling)

    inside = y % 2 == c

    @pl.when(inside)
    def _():
        last_all(15).wait_recv()

    @pl.when(jnp.logical_not(inside))
    def _():
        last_all(16).wait_recv()

    value = jnp.sum(last[...].astype(f32), axis=0) * scale
    mine = pl.ds(lax.axis_index("par") * half, half)
    outs[0] = update[mine] + alpha * direction[mine]
    outs[1] = residual[mine] - alpha * (value + DAMPING * direction[mine])

    each(lambda k: column_all(p, k).wait_send())

    @pl.when(inside)
    def _():
        last_all(15).wait_send()

    @pl.when(jnp.logical_not(inside))
    def _():
        last_all(16).wait_send()


def body(jacobian, energy):
    rows, params = jacobian.shape
    total = rows * lax.axis_size("samp") * lax.axis_size("par")
    tall = params // CHUNKS // LANES
    whole = (params // LANES, LANES)
    piece = (tall // 2, LANES)
    vmem = pl.BlockSpec(memory_space=pltpu.VMEM)
    dma = pltpu.SemaphoreType.DMA
    outs = pl.pallas_call(
        functools.partial(kernel, total),
        out_shape=pltpu.VMEM((2, *piece), f32),
        in_specs=[vmem, pl.BlockSpec(memory_space=pl.ANY)],
        out_specs=vmem,
        scratch_shapes=[
            pltpu.VMEM((rows, params), bf16),
            pltpu.VMEM((params, rows), bf16),
            pltpu.VMEM((tall, LANES), f32),
            pltpu.VMEM((rows, LANES), f32),
            pltpu.VMEM((2, CHUNKS, 2, *piece), bf16),
            pltpu.VMEM((2, CHUNKS, 8, *piece), bf16),
            pltpu.VMEM((2, CHUNKS, 16, *piece), bf16),
            pltpu.VMEM((CHUNKS, *piece), bf16),
            pltpu.VMEM((16, *piece), bf16),
            pltpu.VMEM((8, 1, LANES), f32),
            pltpu.VMEM((16, 1, LANES), f32),
            pltpu.VMEM(whole, f32),
            pltpu.VMEM(whole, f32),
            pltpu.VMEM(whole, f32),
            pltpu.VMEM((2, *whole), f32),
            pltpu.VMEM((2, *piece), f32),
            pltpu.VMEM((8, params // CHUNKS // 2), f32),
            dma((CHUNKS,)),
        ]
        + [dma((2, CHUNKS))] * 6
        + [dma, dma, dma((2,)), dma((2,))],
        compiler_params=pltpu.CompilerParams(
            collective_id=0, has_side_effects=True, vmem_limit_bytes=56 * 2**20
        ),
    )(energy.reshape(-1, LANES), jacobian)
    return outs[0].reshape(-1), outs[1].reshape(-1)


def solution(mesh):
    return jax.shard_map(
        body,
        mesh=mesh,
        in_specs=(P(("samp", "par"), None), P("samp")),
        out_specs=(P("par"), P("par")),
        check_vma=False,
    )
```

time: 71.4 us -> 62.6 us (0.88)
  Pallas kernels: 67.9 us -> 61.2 us
  local copies, waits for them, and re-layouts: 2.59 us -> 0.61 us
    pallas_call x1, Pallas kernels: 67.9 us -> 61.2 us  [body(): pl.pallas_call(functools.partial(kernel, total), out_shape=pltpu.VMEM((2,...]
    unnamed x2 -> x0, local copies, waits for them, and re-layouts: 2.59 us -> none
where the time goes in v2:
time: 62.6 us; the launch traced here: 62.5 us
  Pallas kernels  61.2 us (98%)
  between operations  0.64 us (1%)
    pallas_call x1, Pallas kernels, body(): pl.pallas_call(functools.partial(kernel, total), out_shape=pltpu.VMEM((2,...  61.2 us

profile of v2, /device:TPU:1, one launch (start us, length us, event | category | flops | bytes accessed | tf_op | source)
XLA Modules:
  0.0 62.5 jit_solution(4553004496091153020)
XLA Ops:
  0.6 61.2 %shard_map.41 = f32[2,16,128]{2,1,0:T(8,128)S(1)} custom-call(f32[32,128]{1,0:T(8,128)} %bitcast.5, bf16[512,16384]{1,0:T(8,128)(2,1)} %jac_hbm.1), custom_call_target="tpu_custom_call" | custom-call | tf_op jit(solution)/shard_map/pallas_call | solution.py:307
  61.9 0.6 slice_bitcast_fusion

commit v3 on v2

--- a/solution.py
+++ b/solution.py
@@ -11,7 +11,6 @@
 DAMPING = 0.05
 LANES = 128
 CHUNKS = 4
-VECTOR_TILES = 12
 MESH = pl.DeviceIdType.MESH
 f32, bf16 = jnp.float32, jnp.bfloat16
 
@@ -33,7 +32,7 @@
 def kernel(
     total,
     energy, jac_hbm, outs,
-    jac, jac_t, part, spread, column_out, column, plane, last_out, last, scalar_column, scalar_plane,
+    jac, jac_t, part, column_out, column, plane, last_out, last, scalar_column, scalar_plane,
     update, residual, direction, image, wide, narrow,
     load_sem, column_send, column_recv, plane_send, plane_recv, core_send, core_recv,
     last_send, last_recv, scalar_send, scalar_recv,
@@ -101,36 +100,23 @@
         lax.fori_loop(0, CHUNKS, lambda k, _: (step(k), 0)[1], 0)
 
     def multiply(k, vector):
-        base = pl.multiple_of(k * width, width)
-        split = tall - VECTOR_TILES
-        product = jnp.dot(vector, jac[:, pl.ds(base, split * LANES)], preferred_element_type=f32)
-        for i in range(split):
+        columns = pl.ds(k * width, width)
+        product = jnp.dot(vector, jac[:, columns], preferred_element_type=f32)
+        for i in range(tall):
             part[i : i + 1] = product[:1, i * LANES : (i + 1) * LANES]
-        sums = [jnp.zeros((8, LANES), f32) for _ in range(VECTOR_TILES)]
-        for r in range(0, rows, 8):
-            factor = spread[r : r + 8]
-            for w in range(VECTOR_TILES):
-                columns = pl.ds(base + (split + w) * LANES, LANES)
-                sums[w] += jac[r : r + 8, columns].astype(f32) * factor
-        for w in range(VECTOR_TILES):
-            part[split + w : split + w + 1] = jnp.sum(sums[w], axis=0, keepdims=True)
 
     def transpose(first, count):
         piece = 512
 
         def one(i, _):
-            columns = pl.ds(pl.multiple_of(i * piece, piece), piece)
+            columns = pl.ds(pl.multiple_of(first + i * piece, piece), piece)
             jac_t[columns, :] = jac[:, columns].T
             return 0
 
-        lax.fori_loop(first // piece, (first + count) // piece, one, 0)
+        lax.fori_loop(0, count // piece, one, 0)
 
     def send_columns(p, row, first):
         vector = jnp.broadcast_to(row, (8, rows)).astype(bf16)
-        whole = vector[:1].astype(f32)
-        for i in range(rows // LANES):
-            tile = jnp.broadcast_to(whole[:, i * LANES : (i + 1) * LANES], (LANES, LANES))
-            spread[i * LANES : (i + 1) * LANES] = tile.T
 
         def chunk(k):
             if first:
@@ -142,7 +128,8 @@
             for core, peer in column_peers:
                 column_copy(p, k, core, peer).start()
 
-        each(chunk)
+        for k in range(CHUNKS):
+            chunk(k)
 
     def column_sum(p, k):
         column_all(p, k).wait_recv()
@@ -168,6 +155,8 @@
         return out[0:1] + out[1:2]
 
     def gather(p):
+        lag = 2
+
         def mine(k, inner):
             plane_all(p, k).wait_recv()
             value = jnp.sum(plane[p, k].astype(f32), axis=0)
@@ -179,8 +168,9 @@
             core_copy(p, k).wait_recv()
             return inner + forward(p, k, 1 - c)
 
-        inner = lax.fori_loop(0, CHUNKS, mine, jnp.zeros((1, rows), f32))
-        return lax.fori_loop(0, CHUNKS, theirs, inner)
+        inner = lax.fori_loop(0, lag, mine, jnp.zeros((1, rows), f32))
+        inner = lax.fori_loop(lag, CHUNKS, lambda k, sum: theirs(k - lag, mine(k, sum)), inner)
+        return lax.fori_loop(CHUNKS - lag, CHUNKS, theirs, inner)
 
     def drain(p):
         def chunk(k):
@@ -198,36 +188,43 @@
     deviation = jnp.concatenate(
         [energy[pl.ds(start + i, 1), :] for i in range(rows // LANES)], axis=1
     )
+    update[...] = jnp.zeros(update.shape, f32)
+    direction[...] = jnp.zeros(direction.shape, f32)
     send_columns(0, deviation, True)
-    transpose(0, params // 2)
-    each(functools.partial(send_plane, 0))
-    transpose(params // 2, params // 2)
+
+    def first_plane(k):
+        send_plane(0, k)
+        transpose(k * width, width)
+
+    each(first_plane)
     inner = gather(0)
-    drain(0)
     force = image[0]
     residual[...] = force
-    direction[...] = force
-    update[...] = jnp.zeros(force.shape, f32)
     norm = dot(force, force)
 
+    def settle(p, alpha, beta):
+        update[...] = update[...] + alpha * direction[...]
+        direction[...] = residual[...] + beta * direction[...]
+        drain(p)
+
     def step(it, carry):
-        norm, left, along = carry
+        norm, alpha, beta, left, along = carry
         p = (it + 1) % 2
         send_columns(p, along, False)
+        settle(1 - p, alpha, beta)
         each(functools.partial(send_plane, p))
         inner = gather(p) + DAMPING * along
-        drain(p)
         applied = image[p] + DAMPING * direction[...]
         alpha = norm / dot(direction[...], applied)
-        update[...] = update[...] + alpha * direction[...]
-        residual[...] = residual[...] - alpha * applied
-        new = dot(residual[...], residual[...])
+        rest = residual[...] - alpha * applied
+        residual[...] = rest
+        new = dot(rest, rest)
         beta = new / norm
-        direction[...] = residual[...] + beta * direction[...]
         left = left - alpha * inner
-        return new, left, left + beta * along
-
-    norm, left, along = lax.fori_loop(0, ITERS - 1, step, (norm, inner, inner))
+        return new, alpha, beta, left, left + beta * along
+
+    zero = jnp.zeros((1, 1), f32)
+    norm, alpha, beta, left, along = lax.fori_loop(0, ITERS - 1, step, (norm, zero, zero, inner, inner))
 
     p = ITERS % 2
 
@@ -240,6 +237,7 @@
     for _, peer in column_peers:
         scalar_copy(scalar_column, own, 0, peer).start()
     send_columns(p, along, False)
+    settle(1 - p, alpha, beta)
     scalar_copy(scalar_column, pl.ds(0, 7), 0, sibling).wait()
     scalar_plane[me] = jnp.sum(scalar_column[...], axis=0)
     for peer in plane_peers:
@@ -313,7 +311,6 @@
             pltpu.VMEM((rows, params), bf16),
             pltpu.VMEM((params, rows), bf16),
             pltpu.VMEM((tall, LANES), f32),
-            pltpu.VMEM((rows, LANES), f32),
             pltpu.VMEM((2, CHUNKS, 2, *piece), bf16),
             pltpu.VMEM((2, CHUNKS, 8, *piece), bf16),
             pltpu.VMEM((2, CHUNKS, 16, *piece), bf16),

time: 62.6 us -> 61.1 us (0.976)
  Pallas kernels: 61.2 us -> 59.7 us
    pallas_call x1, Pallas kernels: 61.2 us -> 59.7 us  [body(): pl.pallas_call(functools.partial(kernel, total), out_shape=pltpu.VMEM((2,...]
where the time goes in v3:
time: 61.1 us; the launch traced here: 60.9 us
  Pallas kernels  59.7 us (98%)
  between operations  0.64 us (1%)
    pallas_call x1, Pallas kernels, body(): pl.pallas_call(functools.partial(kernel, total), out_shape=pltpu.VMEM((2,...  59.7 us

profile of v3, /device:TPU:1, one launch (start us, length us, event | category | flops | bytes accessed | tf_op | source)
XLA Modules:
  0.0 60.9 jit_solution(9511649444262617939)
XLA Ops:
  0.6 59.7 %shard_map.41 = f32[2,16,128]{2,1,0:T(8,128)S(1)} custom-call(f32[32,128]{1,0:T(8,128)} %bitcast.5, bf16[512,16384]{1,0:T(8,128)(2,1)} %jac_hbm.1), custom_call_target="tpu_custom_call" | custom-call | tf_op jit(solution)/shard_map/pallas_call | solution.py:305
  60.3 0.6 slice_bitcast_fusion

commit v4 on v3

--- a/solution.py
+++ b/solution.py
@@ -31,11 +31,11 @@
 
 def kernel(
     total,
-    energy, jac_hbm, outs,
-    jac, jac_t, part, column_out, column, plane, last_out, last, scalar_column, scalar_plane,
+    energy_hbm, jac_hbm, outs,
+    energy, jac, jac_t, part, column_out, column, plane, cross, last_out, last, scalar_column, scalar_plane,
     update, residual, direction, image, wide, narrow,
-    load_sem, column_send, column_recv, plane_send, plane_recv, core_send, core_recv,
-    last_send, last_recv, scalar_send, scalar_recv,
+    energy_sem, load_sem, column_send, column_recv, plane_send, plane_recv, core_send, core_recv,
+    cross_send, cross_recv, last_send, last_recv, scalar_send, scalar_recv,
 ):
     rows, params = jac.shape
     width = params // CHUNKS
@@ -55,16 +55,19 @@
     ]
     scale = 1.0 / total
 
-    def load(k):
-        columns = pl.ds(pl.multiple_of(k * width, width), width)
-        return pltpu.make_async_copy(jac_hbm.at[:, columns], jac.at[:, columns], load_sem.at[k])
-
-    for k in range(CHUNKS):
-        load(k).start()
+    def load(i):
+        columns = pl.ds(i * width, width)
+        return pltpu.make_async_copy(jac_hbm.at[:, columns], jac.at[:, columns], load_sem.at[i])
+
+    load_energy = pltpu.make_async_copy(energy_hbm, energy, energy_sem)
+    load_energy.start()
+    for i in range(CHUNKS):
+        load(i).start()
 
     barrier = pltpu.get_barrier_semaphore()
     others = [
-        device((x + a) % 4, (y + b) % 4, z, 1 - c) for a in range(4) for b in range(4) if a or b
+        device((x + a) % 4, (y + b) % 4, z, 1 - c)
+        for a, b in sorted(((a, b) for a in range(4) for b in range(4) if a or b), key=lambda s: hops(*s))
     ]
     greeted = plane_peers + others + [peer for _, peer in column_peers]
     for peer in greeted:
@@ -96,14 +99,17 @@
         piece = image.at[p, pl.ds(k * tall + c * half, half)]
         return copy_to(sibling, piece, piece, core_send.at[p, k], core_recv.at[p, k])
 
+    def cross_copy(slot, source, peer):
+        return copy_to(peer, source, cross.at[slot], cross_send, cross_recv)
+
     def each(step):
         lax.fori_loop(0, CHUNKS, lambda k, _: (step(k), 0)[1], 0)
 
-    def multiply(k, vector):
-        columns = pl.ds(k * width, width)
+    def multiply(k, h, count, vector):
+        columns = pl.ds(k * width + h * width // 2, count * width // 2)
         product = jnp.dot(vector, jac[:, columns], preferred_element_type=f32)
-        for i in range(tall):
-            part[i : i + 1] = product[:1, i * LANES : (i + 1) * LANES]
+        for i in range(count * half):
+            part[h * half + i : h * half + i + 1] = product[:1, i * LANES : (i + 1) * LANES]
 
     def transpose(first, count):
         piece = 512
@@ -115,21 +121,21 @@
 
         lax.fori_loop(0, count // piece, one, 0)
 
-    def send_columns(p, row, first):
+    def send_columns(p, row, first, between=None):
         vector = jnp.broadcast_to(row, (8, rows)).astype(bf16)
-
-        def chunk(k):
+        for k in range(CHUNKS):
             if first:
                 load(k).wait()
-            multiply(k, vector)
+            multiply(k, 0, 2, vector)
             column_out[p, k, 0] = part[:half].astype(bf16)
             column_out[p, k, 1] = part[half:].astype(bf16)
             column[p, k, own] = column_out[p, k, c]
             for core, peer in column_peers:
                 column_copy(p, k, core, peer).start()
-
-        for k in range(CHUNKS):
-            chunk(k)
+            if first and k < CHUNKS - 1:
+                transpose(3 * k * params // 32, 3 * params // 32)
+            if between is not None and k == 0:
+                between()
 
     def column_sum(p, k):
         column_all(p, k).wait_recv()
@@ -154,29 +160,46 @@
         out = jnp.dot(narrow[...].astype(bf16), jac_t[pl.ds(base, depth), :], preferred_element_type=f32)
         return out[0:1] + out[1:2]
 
+    def mine(p, k, inner, exchange=True):
+        plane_all(p, k).wait_recv()
+        value = jnp.sum(plane[p, k].astype(f32), axis=0)
+        image[p, pl.ds(k * tall + c * half, half)] = value * scale
+        if exchange:
+            core_copy(p, k).start()
+        return inner + forward(p, k, c)
+
+    def theirs(p, k, inner):
+        core_copy(p, k).wait_recv()
+        return inner + forward(p, k, 1 - c)
+
     def gather(p):
         lag = 2
-
-        def mine(k, inner):
-            plane_all(p, k).wait_recv()
-            value = jnp.sum(plane[p, k].astype(f32), axis=0)
-            image[p, pl.ds(k * tall + c * half, half)] = value * scale
-            core_copy(p, k).start()
-            return inner + forward(p, k, c)
-
-        def theirs(k, inner):
-            core_copy(p, k).wait_recv()
-            return inner + forward(p, k, 1 - c)
-
-        inner = lax.fori_loop(0, lag, mine, jnp.zeros((1, rows), f32))
-        inner = lax.fori_loop(lag, CHUNKS, lambda k, sum: theirs(k - lag, mine(k, sum)), inner)
-        return lax.fori_loop(CHUNKS - lag, CHUNKS, theirs, inner)
-
-    def drain(p):
+        inner = lax.fori_loop(0, lag, functools.partial(mine, p), jnp.zeros((1, rows), f32))
+        inner = lax.fori_loop(
+            lag, CHUNKS, lambda k, sum: theirs(p, k - lag, mine(p, k, sum)), inner
+        )
+        return lax.fori_loop(CHUNKS - lag, CHUNKS, functools.partial(theirs, p), inner)
+
+    def gather_first(p):
+        k = CHUNKS - 1
+        inner = mine(p, 0, jnp.zeros((1, rows), f32))
+        inner = lax.fori_loop(1, k, lambda k, sum: theirs(p, k - 1, mine(p, k, sum)), inner)
+        inner = mine(p, k, inner, False)
+        inner = theirs(p, k - 1, inner)
+        everything = pl.ds(0, 16)
+        cross_copy(everything, cross.at[everything], sibling).wait()
+        value = jnp.sum(cross[...].astype(f32), axis=0)
+        image[p, pl.ds(k * tall + (1 - c) * half, half)] = value * scale
+        return inner + forward(p, k, 1 - c)
+
+    def drain(p, whole):
         def chunk(k):
             column_all(p, k).wait_send()
             plane_all(p, k).wait_send()
-            core_copy(p, k).wait_send()
+
+            @pl.when(jnp.logical_or(k < CHUNKS - 1, whole))
+            def _():
+                core_copy(p, k).wait_send()
 
         each(chunk)
 
@@ -184,6 +207,7 @@
         return jnp.sum(a * b, keepdims=True)
 
     narrow[...] = jnp.zeros(narrow.shape, f32)
+    load_energy.wait()
     start = lax.axis_index("par") * (rows // LANES)
     deviation = jnp.concatenate(
         [energy[pl.ds(start + i, 1), :] for i in range(rows // LANES)], axis=1
@@ -192,26 +216,32 @@
     direction[...] = jnp.zeros(direction.shape, f32)
     send_columns(0, deviation, True)
 
-    def first_plane(k):
-        send_plane(0, k)
-        transpose(k * width, width)
-
-    each(first_plane)
-    inner = gather(0)
+    piece = params // 32
+    send_plane(0, 0)
+    transpose(9 * piece, 5 * piece)
+    send_plane(0, 1)
+    transpose(14 * piece, 5 * piece)
+    send_plane(0, 2)
+    transpose(19 * piece, 5 * piece)
+    send_plane(0, 3)
+    for peer in others + [sibling]:
+        cross_copy(me, plane.at[0, 3, me], peer).start()
+    transpose(24 * piece, 8 * piece)
+    inner = gather_first(0)
     force = image[0]
     residual[...] = force
     norm = dot(force, force)
 
-    def settle(p, alpha, beta):
+    def settle(p, alpha, beta, whole):
         update[...] = update[...] + alpha * direction[...]
         direction[...] = residual[...] + beta * direction[...]
-        drain(p)
+        drain(p, whole)
 
     def step(it, carry):
         norm, alpha, beta, left, along = carry
         p = (it + 1) % 2
         send_columns(p, along, False)
-        settle(1 - p, alpha, beta)
+        settle(1 - p, alpha, beta, it > 0)
         each(functools.partial(send_plane, p))
         inner = gather(p) + DAMPING * along
         applied = image[p] + DAMPING * direction[...]
@@ -232,12 +262,14 @@
         piece = buffer.at[slot]
         return copy_to(peer, piece, piece, scalar_send.at[stage], scalar_recv.at[stage])
 
-    squares = dot(along.astype(bf16).astype(f32), along)
-    scalar_column[own] = jnp.broadcast_to(squares, (1, LANES))
-    for _, peer in column_peers:
-        scalar_copy(scalar_column, own, 0, peer).start()
-    send_columns(p, along, False)
-    settle(1 - p, alpha, beta)
+    def send_squares():
+        squares = dot(along.astype(bf16).astype(f32), along)
+        scalar_column[own] = jnp.broadcast_to(squares, (1, LANES))
+        for _, peer in column_peers:
+            scalar_copy(scalar_column, own, 0, peer).start()
+
+    send_columns(p, along, False, send_squares)
+    settle(1 - p, alpha, beta, True)
     scalar_copy(scalar_column, pl.ds(0, 7), 0, sibling).wait()
     scalar_plane[me] = jnp.sum(scalar_column[...], axis=0)
     for peer in plane_peers:
@@ -305,15 +337,17 @@
     outs = pl.pallas_call(
         functools.partial(kernel, total),
         out_shape=pltpu.VMEM((2, *piece), f32),
-        in_specs=[vmem, pl.BlockSpec(memory_space=pl.ANY)],
+        in_specs=[pl.BlockSpec(memory_space=pltpu.HBM)] * 2,
         out_specs=vmem,
         scratch_shapes=[
+            pltpu.VMEM((energy.shape[0] // LANES, LANES), f32),
             pltpu.VMEM((rows, params), bf16),
             pltpu.VMEM((params, rows), bf16),
             pltpu.VMEM((tall, LANES), f32),
             pltpu.VMEM((2, CHUNKS, 2, *piece), bf16),
             pltpu.VMEM((2, CHUNKS, 8, *piece), bf16),
             pltpu.VMEM((2, CHUNKS, 16, *piece), bf16),
+            pltpu.VMEM((16, *piece), bf16),
             pltpu.VMEM((CHUNKS, *piece), bf16),
             pltpu.VMEM((16, *piece), bf16),
             pltpu.VMEM((8, 1, LANES), f32),
@@ -324,10 +358,11 @@
             pltpu.VMEM((2, *whole), f32),
             pltpu.VMEM((2, *piece), f32),
             pltpu.VMEM((8, params // CHUNKS // 2), f32),
+            dma,
             dma((CHUNKS,)),
         ]
         + [dma((2, CHUNKS))] * 6
-        + [dma, dma, dma((2,)), dma((2,))],
+        + [dma, dma, dma, dma, dma((2,)), dma((2,))],
         compiler_params=pltpu.CompilerParams(
             collective_id=0, has_side_effects=True, vmem_limit_bytes=56 * 2**20
         ),

time: 61.1 us -> 59.9 us (0.980)
  Pallas kernels: 59.7 us -> 58.5 us
    pallas_call x1, Pallas kernels: 59.7 us -> 58.5 us  [body(): pl.pallas_call(functools.partial(kernel, total), out_shape=pltpu.VMEM((2,...]
where the time goes in v4:
time: 59.9 us; the launch traced here: 59.8 us
  Pallas kernels  58.5 us (98%)
  between operations  0.64 us (1%)
  local copies, waits for them, and re-layouts  0.61 us (1%)
    pallas_call x1, Pallas kernels, body(): pl.pallas_call(functools.partial(kernel, total), out_shape=pltpu.VMEM((2,...  58.5 us

profile of v4, /device:TPU:1, one launch (start us, length us, event | category | flops | bytes accessed | tf_op | source)
XLA Modules:
  0.0 59.8 jit_solution(13197803954870553163)
XLA Ops:
  0.6 58.5 %shard_map.41 = f32[2,16,128]{2,1,0:T(8,128)S(1)} custom-call(f32[32,128]{1,0:T(8,128)} %bitcast.5, bf16[512,16384]{1,0:T(8,128)(2,1)} %jac_hbm.1), custom_call_target="tpu_custom_call" | custom-call | tf_op jit(solution)/shard_map/pallas_call | solution.py:337
  59.1 0.6 %slice_bitcast_fusion = (f32[2048]{0:T(1024)}, f32[2048]{0:T(1024)}) fusion(f32[2,16,128]{2,1,0:T(8,128)S(1)} %shard_map.41), kind=kLoop, calls=%fused_computation | loop fusion | bytes 32768 | tf_op jit(solution)/shard_map/reshape;squeeze | solution.py:370

commit v5 on v4

--- a/solution.py
+++ b/solution.py
@@ -61,7 +61,7 @@
 
     load_energy = pltpu.make_async_copy(energy_hbm, energy, energy_sem)
     load_energy.start()
-    for i in range(CHUNKS):
+    for i in range(2):
         load(i).start()
 
     barrier = pltpu.get_barrier_semaphore()
@@ -126,14 +126,14 @@
         for k in range(CHUNKS):
             if first:
                 load(k).wait()
+                if k + 2 < CHUNKS:
+                    load(k + 2).start()
             multiply(k, 0, 2, vector)
             column_out[p, k, 0] = part[:half].astype(bf16)
             column_out[p, k, 1] = part[half:].astype(bf16)
             column[p, k, own] = column_out[p, k, c]
             for core, peer in column_peers:
                 column_copy(p, k, core, peer).start()
-            if first and k < CHUNKS - 1:
-                transpose(3 * k * params // 32, 3 * params // 32)
             if between is not None and k == 0:
                 between()
 
@@ -146,7 +146,7 @@
         for peer in plane_peers:
             plane_copy(p, k, me, peer).start()
 
-    def forward(p, k, h):
+    def forward(p, k, h, transposed=True):
         value = image[p, pl.ds(k * tall + h * half, half)]
         high = value.astype(bf16).astype(f32)
         wide[0] = high
@@ -157,20 +157,26 @@
             narrow[1:2, columns] = wide[1, i : i + 1]
         depth = width // 2
         base = pl.multiple_of(k * width + h * depth, depth)
-        out = jnp.dot(narrow[...].astype(bf16), jac_t[pl.ds(base, depth), :], preferred_element_type=f32)
+        terms = narrow[...].astype(bf16)
+        if transposed:
+            out = jnp.dot(terms, jac_t[pl.ds(base, depth), :], preferred_element_type=f32)
+        else:
+            out = lax.dot_general(
+                terms, jac[:, pl.ds(base, depth)], (((1,), (1,)), ((), ())), preferred_element_type=f32
+            )
         return out[0:1] + out[1:2]
 
-    def mine(p, k, inner, exchange=True):
+    def mine(p, k, inner, exchange=True, transposed=True):
         plane_all(p, k).wait_recv()
         value = jnp.sum(plane[p, k].astype(f32), axis=0)
         image[p, pl.ds(k * tall + c * half, half)] = value * scale
         if exchange:
             core_copy(p, k).start()
-        return inner + forward(p, k, c)
-
-    def theirs(p, k, inner):
+        return inner + forward(p, k, c, transposed)
+
+    def theirs(p, k, inner, transposed=True):
         core_copy(p, k).wait_recv()
-        return inner + forward(p, k, 1 - c)
+        return inner + forward(p, k, 1 - c, transposed)
 
     def gather(p):
         lag = 2
@@ -182,8 +188,11 @@
 
     def gather_first(p):
         k = CHUNKS - 1
-        inner = mine(p, 0, jnp.zeros((1, rows), f32))
-        inner = lax.fori_loop(1, k, lambda k, sum: theirs(p, k - 1, mine(p, k, sum)), inner)
+        inner = mine(p, 0, jnp.zeros((1, rows), f32), True, False)
+        inner = mine(p, 1, inner, True, False)
+        inner = theirs(p, 0, inner, False)
+        inner = mine(p, 2, inner)
+        inner = theirs(p, 1, inner, False)
         inner = mine(p, k, inner, False)
         inner = theirs(p, k - 1, inner)
         everything = pl.ds(0, 16)
@@ -216,17 +225,17 @@
     direction[...] = jnp.zeros(direction.shape, f32)
     send_columns(0, deviation, True)
 
-    piece = params // 32
+    piece = width // 2
     send_plane(0, 0)
-    transpose(9 * piece, 5 * piece)
+    transpose(2 * width + 0 * piece, piece)
     send_plane(0, 1)
-    transpose(14 * piece, 5 * piece)
+    transpose(2 * width + 1 * piece, piece)
     send_plane(0, 2)
-    transpose(19 * piece, 5 * piece)
+    transpose(2 * width + 2 * piece, piece)
     send_plane(0, 3)
     for peer in others + [sibling]:
         cross_copy(me, plane.at[0, 3, me], peer).start()
-    transpose(24 * piece, 8 * piece)
+    transpose(2 * width + 3 * piece, piece)
     inner = gather_first(0)
     force = image[0]
     residual[...] = force
@@ -242,7 +251,17 @@
         p = (it + 1) % 2
         send_columns(p, along, False)
         settle(1 - p, alpha, beta, it > 0)
+
+        @pl.when(it == 0)
+        def _():
+            transpose(0, width)
+
         each(functools.partial(send_plane, p))
+
+        @pl.when(it == 0)
+        def _():
+            transpose(width, width)
+
         inner = gather(p) + DAMPING * along
         applied = image[p] + DAMPING * direction[...]
         alpha = norm / dot(direction[...], applied)

time: 59.9 us -> 59.4 us (level)
  no operation moved by 1% of the time
where the time goes in v5:
time: 59.4 us; the launch traced here: 59.3 us
  Pallas kernels  58 us (98%)
  between operations  0.64 us (1%)
  local copies, waits for them, and re-layouts  0.61 us (1%)
    pallas_call x1, Pallas kernels, body(): pl.pallas_call(functools.partial(kernel, total), out_shape=pltpu.VMEM((2,...  58 us

profile of v5, /device:TPU:1, one launch (start us, length us, event | category | flops | bytes accessed | tf_op | source)
XLA Modules:
  0.0 59.3 jit_solution(18429100832835227751)
XLA Ops:
  0.6 58.0 %shard_map.41 = f32[2,16,128]{2,1,0:T(8,128)S(1)} custom-call(f32[32,128]{1,0:T(8,128)} %bitcast.5, bf16[512,16384]{1,0:T(8,128)(2,1)} %jac_hbm.1), custom_call_target="tpu_custom_call" | custom-call | tf_op jit(solution)/shard_map/pallas_call | solution.py:356
  58.7 0.6 %slice_bitcast_fusion = (f32[2048]{0:T(1024)}, f32[2048]{0:T(1024)}) fusion(f32[2,16,128]{2,1,0:T(8,128)S(1)} %shard_map.41), kind=kLoop, calls=%fused_computation | loop fusion | bytes 32768 | tf_op jit(solution)/shard_map/reshape;squeeze | solution.py:389

commit v6 on v5

--- a/solution.py
+++ b/solution.py
@@ -179,12 +179,14 @@
         return inner + forward(p, k, 1 - c, transposed)
 
     def gather(p):
-        lag = 2
-        inner = lax.fori_loop(0, lag, functools.partial(mine, p), jnp.zeros((1, rows), f32))
-        inner = lax.fori_loop(
-            lag, CHUNKS, lambda k, sum: theirs(p, k - lag, mine(p, k, sum)), inner
-        )
-        return lax.fori_loop(CHUNKS - lag, CHUNKS, functools.partial(theirs, p), inner)
+        inner = jnp.zeros((1, rows), f32)
+        lag = 1
+        for k in range(CHUNKS + lag):
+            if k < CHUNKS:
+                inner = mine(p, k, inner)
+            if k >= lag:
+                inner = theirs(p, k - lag, inner)
+        return inner
 
     def gather_first(p):
         k = CHUNKS - 1
@@ -256,7 +258,8 @@
         def _():
             transpose(0, width)
 
-        each(functools.partial(send_plane, p))
+        for k in range(CHUNKS):
+            send_plane(p, k)
 
         @pl.when(it == 0)
         def _():

time: 59.4 us -> 58.1 us (0.978)
  Pallas kernels: 58 us -> 56.8 us
    pallas_call x1, Pallas kernels: 58 us -> 56.8 us  [body(): pl.pallas_call(functools.partial(kernel, total), out_shape=pltpu.VMEM((2,...]
where the time goes in v6:
time: 58.1 us; the launch traced here: 58 us
  Pallas kernels  56.8 us (98%)
  between operations  0.64 us (1%)
  local copies, waits for them, and re-layouts  0.61 us (1%)
    pallas_call x1, Pallas kernels, body(): pl.pallas_call(functools.partial(kernel, total), out_shape=pltpu.VMEM((2,...  56.8 us

profile of v6, /device:TPU:1, one launch (start us, length us, event | category | flops | bytes accessed | tf_op | source)
XLA Modules:
  0.0 58.0 jit_solution(12827028102018672764)
XLA Ops:
  0.6 56.8 %shard_map.41 = f32[2,16,128]{2,1,0:T(8,128)S(1)} custom-call(f32[32,128]{1,0:T(8,128)} %bitcast.5, bf16[512,16384]{1,0:T(8,128)(2,1)} %jac_hbm.1), custom_call_target="tpu_custom_call" | custom-call | tf_op jit(solution)/shard_map/pallas_call | solution.py:359
  57.4 0.6 %slice_bitcast_fusion = (f32[2048]{0:T(1024)}, f32[2048]{0:T(1024)}) fusion(f32[2,16,128]{2,1,0:T(8,128)S(1)} %shard_map.41), kind=kLoop, calls=%fused_computation | loop fusion | bytes 32768 | tf_op jit(solution)/shard_map/reshape;squeeze | solution.py:392

commit v7 on v6

--- a/solution.py
+++ b/solution.py
@@ -33,7 +33,7 @@
     total,
     energy_hbm, jac_hbm, outs,
     energy, jac, jac_t, part, column_out, column, plane, cross, last_out, last, scalar_column, scalar_plane,
-    update, residual, direction, image, wide, narrow,
+    update, residual, direction, image, narrow,
     energy_sem, load_sem, column_send, column_recv, plane_send, plane_recv, core_send, core_recv,
     cross_send, cross_recv, last_send, last_recv, scalar_send, scalar_recv,
 ):
@@ -149,12 +149,11 @@
     def forward(p, k, h, transposed=True):
         value = image[p, pl.ds(k * tall + h * half, half)]
         high = value.astype(bf16).astype(f32)
-        wide[0] = high
-        wide[1] = value - high
+        low = value - high
         for i in range(half):
             columns = slice(i * LANES, (i + 1) * LANES)
-            narrow[0:1, columns] = wide[0, i : i + 1]
-            narrow[1:2, columns] = wide[1, i : i + 1]
+            narrow[0:1, columns] = high[i : i + 1]
+            narrow[1:2, columns] = low[i : i + 1]
         depth = width // 2
         base = pl.multiple_of(k * width + h * depth, depth)
         terms = narrow[...].astype(bf16)
@@ -378,7 +377,6 @@
             pltpu.VMEM(whole, f32),
             pltpu.VMEM(whole, f32),
             pltpu.VMEM((2, *whole), f32),
-            pltpu.VMEM((2, *piece), f32),
             pltpu.VMEM((8, params // CHUNKS // 2), f32),
             dma,
             dma((CHUNKS,)),

time: 58.1 us -> 58.2 us (level)
  no operation moved by 1% of the time
where the time goes in v7:
time: 58.2 us; the launch traced here: 58.1 us
  Pallas kernels  56.8 us (98%)
  between operations  0.64 us (1%)
  local copies, waits for them, and re-layouts  0.61 us (1%)
    pallas_call x1, Pallas kernels, body(): pl.pallas_call(functools.partial(kernel, total), out_shape=pltpu.VMEM((2,...  56.8 us

profile of v7, /device:TPU:1, one launch (start us, length us, event | category | flops | bytes accessed | tf_op | source)
XLA Modules:
  0.0 58.1 jit_solution(16512418590142134040)
XLA Ops:
  0.6 56.8 %shard_map.41 = f32[2,16,128]{2,1,0:T(8,128)S(1)} custom-call(f32[32,128]{1,0:T(8,128)} %bitcast.5, bf16[512,16384]{1,0:T(8,128)(2,1)} %jac_hbm.1), custom_call_target="tpu_custom_call" | custom-call | tf_op jit(solution)/shard_map/pallas_call | solution.py:358
  57.5 0.6 %slice_bitcast_fusion = (f32[2048]{0:T(1024)}, f32[2048]{0:T(1024)}) fusion(f32[2,16,128]{2,1,0:T(8,128)S(1)} %shard_map.41), kind=kLoop, calls=%fused_computation | loop fusion | bytes 32768 | tf_op jit(solution)/shard_map/reshape;squeeze | solution.py:390
